TPU v7x, 256 devices: a whole 4x4x8 slice. The times are simulated.
256 devices in a mesh: row: 8 (over y, x_hi), col: 32 (over z, x_lo, core).
Axes of the slice: x: 4 (x_hi: 2, x_lo: 2; x = x_hi * 2 + x_lo), y: 4, z: 8, core: 2. Of those that a mesh axis runs over, the one named last changes fastest.
Arguments:
- gradient: bfloat16 [8192, 8192], P('row', 'col'), may hold values from -0.6 to 0.6
- left_old: float32 [8192, 8192], P('row', 'col'), may hold values from -6 to 6
- right_old: float32 [8192, 8192], P('row', 'col'), may hold values from -6 to 6
Outputs:
- left_factor: float32 [8192, 8192], P('row', 'col')
- right_factor: float32 [8192, 8192], P('row', 'col')
All inputs are finite; a program needn't handle non-finite values.
Results may differ from a plain program's by a relative error of at most 0.0003.
Values may be sent and summed in bfloat16 or wider, within the bound.
A program may use at most 128 MiB of HBM per device.

v0:
```python
import jax
import jax.numpy as jnp
from jax import lax
from jax.sharding import PartitionSpec as P


def broadcast(block, axis, owner):
    block = jnp.where(lax.axis_index(axis) == owner, block, jnp.zeros_like(block))
    return lax.psum(block, axis)


def on_device(gradient, left_old, right_old):
    panel = lax.all_gather(gradient, "col", axis=1, tiled=True)
    row_count = lax.axis_size("row")
    col_count = lax.axis_size("col")
    per_group = col_count // row_count
    block_rows = gradient.shape[0] // per_group
    col_place = lax.axis_index("col")
    mine = lax.dynamic_slice_in_dim(panel, col_place % per_group * block_rows, block_rows, 0)
    partner = broadcast(mine, "row", col_place // per_group)
    gram_left = lax.dot_general(
        panel, partner, (((1,), (1,)), ((), ())), preferred_element_type=jnp.float32
    )
    left_factor = 0.95 * left_old + 0.05 * gram_left
    gram_right = lax.psum_scatter(
        lax.dot_general(
            panel, gradient, (((0,), (0,)), ((), ())), preferred_element_type=jnp.float32
        ),
        "row",
        scatter_dimension=0,
        tiled=True,
    )
    right_factor = 0.95 * right_old + 0.05 * gram_right
    return (left_factor, right_factor)


def solution(mesh):
    placed = (P("row", "col"), P("row", "col"), P("row", "col"))
    return jax.shard_map(
        on_device,
        mesh=mesh,
        in_specs=placed,
        out_specs=(P("row", "col"), P("row", "col")),
        check_vma=False,
    )
```

profile of v0, /device:TPU:16, one launch (start us, length us, event | category | flops | bytes accessed | tf_op | source)
XLA Modules:
  0.0 460.6 jit_solution(15480675786045124043)
XLA Ops:
  7.2 0.0 copy-start.2
  7.2 0.0 all-gather.2.cloned.1.call-start
  7.2 0.7 all-gather.2.cloned.1.call-update
  7.9 0.0 all-reduce.2.cloned.1.call-start
  8.0 128.7 %all-gather.2.cloned.1.call-done = bf16[1024,8192]{1,0:T(8,128)(2,1)} async-done(((bf16[1024,256]{1,0:T(8,128)(2,1)}), bf16[1024,8192]{1,0:T(8,128)(2,1)}) %all-gather.2.cloned.1.call-update) | async-done | bytes 16777232 | tf_op jit(solution)/shard_map/all_gather | solution.py:13
  136.7 4.9 %dynamic-slice_select_fusion = bf16[256,8192]{1,0:T(8,128)(2,1)} fusion(bf16[1024,8192]{1,0:T(8,128)(2,1)} %all-gather.2.cloned.1.call-done, s32[]{:T(128)S(6)} %select_n.25, pred[]{:T(512)S(6)} %eq.5), kind=kLoop, calls=%fused_computation | loop fusion | flops 2097152 | bytes 8388613 | tf_op jit(solution)/shard_map/jit(_where)/select_n | solution.py:8
  141.7 0.0 all-reduce.2.cloned.1.call-update
  141.7 0.0 reduce-scatter.2.cloned.1.call-start
  141.8 0.0 copy-done.2
  141.8 12.7 %fusion.2 = f32[8192,256]{0,1:T(8,128)} fusion(bf16[1024,8192]{1,0:T(8,128)(2,1)} %all-gather.2.cloned.1.call-done, bf16[1024,256]{1,0:T(8,128)(2,1)S(1)} %copy-done.2), kind=kOutput, calls=%fused_computation.5 | convolution fusion | flops 4294967296 | bytes 25690112 | tf_op jit(solution)/shard_map/dot_general | solution.py:26
  154.5 0.0 copy-start
  154.5 0.0 copy-start.1
  154.5 0.0 reduce-scatter.2.cloned.1.call-update
  154.5 1.2 copy-done
  155.7 0.3 copy.5
  156.0 0.0 copy-done.1
  156.0 0.3 copy.6
  156.4 172.7 %all-reduce.2.cloned.1.call-done = bf16[256,8192]{1,0:T(8,128)(2,1)} async-done(((bf16[256,8192]{1,0:T(8,128)(2,1)}), bf16[256,8192]{1,0:T(8,128)(2,1)}) %all-reduce.2.cloned.1.call-update) | async-done | bytes 4194320 | tf_op jit(solution)/shard_map/psum | solution.py:9
  329.1 9.3 %fusion.1 = f32[1024,256]{0,1:T(8,128)S(1)} fusion(bf16[256,8192]{1,0:T(8,128)(2,1)} %all-reduce.2.cloned.1.call-done, bf16[1024,8192]{1,0:T(8,128)(2,1)} %all-gather.2.cloned.1.call-done, f32[1024,256]{0,1:T(8,128)S(1)} %copy.5), kind=kOutput, calls=%fused_computation.3 | convolution fusion | flops 4295753728 | bytes 23068672 | tf_op jit(solution)/shard_map/dot_general | solution.py:21
  338.4 1.3 copy.8
  339.7 111.7 %reduce-scatter.2.cloned.1.call-done = f32[1024,256]{0,1:T(8,128)} async-done(((f32[8192,256]{0,1:T(8,128)}), f32[1024,256]{0,1:T(8,128)}) %reduce-scatter.2.cloned.1.call-update) | async-done | bytes 1048592 | tf_op jit(solution)/shard_map/reduce_scatter | solution.py:25
  451.4 1.4 multiply_add_fusion
  452.8 1.3 copy.9
Async XLA Ops:
  7.2 134.6 %copy-start.2 = (bf16[1024,256]{1,0:T(8,128)(2,1)S(1)}, bf16[1024,256]{1,0:T(8,128)(2,1)}, u32[]{:S(2)}) copy-start(bf16[1024,256]{1,0:T(8,128)(2,1)} %param.3) | copy-start | bytes 1572868
  7.2 129.6 %all-gather.2.cloned.1.call-start = ((), (), s32[]{:S(2)}) async-start(), calls=%async_computation.1 | async-start | bytes 17301504 | tf_op jit(solution)/shard_map/all_gather | solution.py:13
  7.9 321.2 %all-reduce.2.cloned.1.call-start = ((), (), s32[]{:S(2)}) async-start(), calls=%async_computation.2 | async-start | bytes 8388608 | tf_op jit(solution)/shard_map/psum | solution.py:9
  141.7 309.7 %reduce-scatter.2.cloned.1.call-start = ((), (), s32[]{:S(2)}) async-start(), calls=%async_computation.3 | async-start | bytes 9437184 | tf_op jit(solution)/shard_map/reduce_scatter | solution.py:25
  154.5 1.2 copy-start
  154.5 1.6 copy-start.1
Sparse Core Ops, SparseCore 0:
  9.8 126.9 all-gather.1
  141.8 187.1 all-reduce.1
  333.2 118.1 reduce-scatter.1
where the time goes:
time: 463 us; the launch traced here: 461 us
  waiting for transfers between devices  414 us (89%)
  matrix products  22.1 us (5%)
  between operations  13.8 us (3%)
  other arithmetic  6.38 us (1%)
    psum x1, waiting for transfers between devices, broadcast(): return lax.psum(block, axis)  173 us
    all_gather x1, waiting for transfers between devices, on_device(): panel = lax.all_gather(gradient, 'col', axis=1, tiled=True)  129 us
    reduce_scatter x1, waiting for transfers between devices, on_device(): lax.psum_scatter(lax.dot_general(panel, gradient, (((0,), (0,)), ((), ())...  112 us
    dot_general x1, matrix products, on_device(): lax.dot_general(panel, gradient, (((0,), (0,)), ((), ())), preferred_elem...  12.7 us
    dot_general x1, matrix products, on_device(): lax.dot_general(panel, partner, (((1,), (1,)), ((), ())), preferred_eleme...  9.35 us
  transfers between devices with their start and end apart: 3, of which 3 were waited for; matrix products, arithmetic and copies ran while one was open for 5% of the time, Pallas kernels for 0%

commit v1 on v0

v1 whole, which is shorter than its diff:
```python
import jax
import jax.numpy as jnp
from jax import lax
from jax.experimental import pallas as pl
from jax.experimental.pallas import tpu as pltpu
from jax.sharding import PartitionSpec as P

MESH = pl.DeviceIdType.MESH
BF16, F32 = jnp.bfloat16, jnp.float32
ROW = 1024
SUB = 256
RING = 8
DEPTH = RING * SUB
CHUNK = 16
STEPS = 512 // CHUNK
HALF = STEPS // 2
LAG = 3
ADD, END = 3, 8


def at(start, size):
    return pl.ds(pl.multiple_of(start, size), size)


def kernel(g_ref, lo_ref, ro_ref, l_ref, r_ref,
           grad, turned, own, rec, prod_l, prod_r, core_l, core_r, chip_l, chip_r, last_l, last_r, total, old, out,
           load_sem, swap_send, swap_recv, mix_send, mix_recv, ag_send, ag_recv, bc_send, bc_recv, own_sem,
           core_send, core_recv, chip_send, chip_recv, out_sem):
    a, j = lax.axis_index("row"), lax.axis_index("col")
    y, h = a // 2, a % 2
    z, l, c = j // 4, (j // 2) % 2, j % 2
    p = jnp.where(h == 0, y, 7 - y)
    mine = l * 2 + c

    def plane(step):
        q = (p + step + RING) % RING
        h2 = q // 4
        y2 = jnp.where(h2 == 0, q, 7 - q)
        return (y2 * 2 + h2, z * 4 + ((l + h + h2) % 2) * 2 + c)

    def line(step):
        return (a, ((z + step + RING) % RING) * 4 + mine)

    def inside(dl, dc):
        return (a, z * 4 + ((l + dl) % 2) * 2 + (c + dc) % 2)

    sides = (line(1), line(-1), plane(1), plane(-1))
    mate, twin = inside(0, 1), inside(1, 0)

    grad_in = pltpu.make_async_copy(g_ref, grad, load_sem.at[0])
    grad_in.start()
    old_in = [pltpu.make_async_copy(ref, old.at[q], load_sem.at[1 + q]) for q, ref in enumerate((lo_ref, ro_ref))]
    for copy in old_in:
        copy.start()

    barrier = pltpu.get_barrier_semaphore()
    for device in sides + (mate, twin, inside(1, 1)):
        pl.semaphore_signal(barrier, inc=1, device_id=device, device_id_type=MESH)
    pl.semaphore_wait(barrier, 7)

    def swap(u):
        rows = pl.ds(u * SUB, SUB)
        return pltpu.make_async_remote_copy(
            src_ref=g_ref.at[rows], dst_ref=own.at[0, rows, at(z * SUB, SUB)],
            send_sem=swap_send.at[u], recv_sem=swap_recv.at[u], device_id=twin, device_id_type=MESH)

    for u in range(4):
        @pl.when(h == 0)
        def _():
            rows = pl.ds(u * SUB, SUB)
            pltpu.make_async_copy(g_ref.at[rows], own.at[0, rows, at(z * SUB, SUB)], swap_recv.at[u]).start()

        @pl.when(h == 1)
        def _():
            swap(u).start()

    grad_in.wait()
    for u in range(4):
        turned[:, u * SUB:(u + 1) * SUB] = grad[u * SUB:(u + 1) * SUB, :].T

    def mix(dl, dc):
        part = ((l + dl + h) % 2) * 2 + (c + dc) % 2
        src = turned.at[:, at(part * SUB, SUB)]
        dst = own.at[1, at(mine * SUB, SUB), at(a * SUB, SUB)]
        if dl == dc == 0:
            return pltpu.make_async_copy(src, dst, mix_recv.at[mine])
        return pltpu.make_async_remote_copy(
            src_ref=src, dst_ref=dst, send_sem=mix_send.at[dl * 2 + dc], recv_sem=mix_recv.at[mine],
            device_id=inside(dl, dc), device_id_type=MESH)

    for dl, dc in ((1, 0), (1, 1), (0, 1), (0, 0)):
        mix(dl, dc).start()

    def gather(r, q):
        prob, sign = r // 2, 1 - 2 * (r % 2)
        step = q // 4
        u = (q + 2 * (r % 2)) % 4
        if prob == 0:
            k = (z - sign * step + RING) % RING
        else:
            k = (p - sign * step + RING) % RING
            k = jnp.where(k < 4, 2 * k, 15 - 2 * k)
        part = own.at[prob, at(u * SUB, SUB), at(k * SUB, SUB)]
        return pltpu.make_async_remote_copy(
            src_ref=part, dst_ref=part, send_sem=ag_send.at[r], recv_sem=ag_recv.at[r, q],
            device_id=sides[r], device_id_type=MESH)

    for u in range(4):
        rows = pl.ds(u * SUB, SUB)
        here = own.at[0, rows, at(z * SUB, SUB)]
        pltpu.make_async_copy(here, here, swap_recv.at[u]).wait()
        gather(0, u).start()
        gather(1, (u + 2) % 4).start()
    for u in range(4):
        rows = pl.ds(u * SUB, SUB)
        here = own.at[1, rows, at(a * SUB, SUB)]
        pltpu.make_async_copy(here, here, mix_recv.at[u]).wait()
        gather(2, u).start()
        gather(3, (u + 2) % 4).start()

    @pl.loop(4, 14)
    def _(q):
        for r in range(4):
            gather(r, q - 4).wait_recv()
            gather(r, q).start()

    @pl.loop(10, 14)
    def _(q):
        for r in range(4):
            gather(r, q).wait_recv()

    for copy in old_in:
        copy.wait()

    first = jnp.where(z % 2 == 0, z // 2, 7 - z // 2)
    away = ((p - first + RING) % RING, (first - p + RING) % RING, (z - a + RING) % RING, (a - z + RING) % RING)
    onward = (sides[2], sides[3], sides[0], sides[1])

    def own_copy(prob, g, s):
        src = s * SUB + g * 64 if prob == 0 else g * SUB + s * 64
        return pltpu.make_async_copy(own.at[prob, at(src, 64)], rec.at[prob, at(g * SUB + s * 64, 64)], own_sem.at[prob])

    for prob in range(2):
        @pl.when(away[prob * 2] == 0)
        def _():
            @pl.loop(0, 16)
            def _(n):
                own_copy(prob, n // 4, n % 4).start()

    prods, cores, chips, lasts = (prod_l, prod_r), (core_l, core_r), (chip_l, chip_r), (last_l, last_r)

    def to_mate(prob, g):
        return pltpu.make_async_remote_copy(
            src_ref=prods[prob].at[g, 1 - c], dst_ref=cores[prob].at[g],
            send_sem=core_send.at[prob, g], recv_sem=core_recv.at[prob, g], device_id=mate, device_id_type=MESH)

    def to_twin(prob, g):
        return pltpu.make_async_remote_copy(
            src_ref=chips[prob].at[g], dst_ref=lasts[prob].at[g],
            send_sem=chip_send.at[prob, g], recv_sem=chip_recv.at[prob, g], device_id=twin, device_id_type=MESH)

    def out_copy(prob, n):
        if prob == 0:
            cols = pl.ds(n * 128, 128)
            return pltpu.make_async_copy(out.at[0, :, cols], l_ref.at[:, cols], out_sem.at[0, n])
        rows = at(n * SUB, SUB)
        return pltpu.make_async_copy(out.at[1, rows], r_ref.at[rows], out_sem.at[1, n])

    def multiply(prob, g):
        @pl.loop(0, 4)
        def _(n):
            tile = lax.dot_general(
                rec[prob, at(g * SUB, SUB), :], own[prob, at(n * SUB, SUB), :],
                (((1,), (1,)), ((), ())), preferred_element_type=F32)
            if prob == 0:
                for s in range(4):
                    prod_l[g, s % 2, s // 2, :, at(n * SUB, SUB)] = tile[s * 64:(s + 1) * 64, :]
            else:
                prod_r[g, n % 2, n // 2] = tile
        to_mate(prob, g).start()

    def add(prob, g):
        to_mate(prob, g).wait_recv()
        chips[prob][g] = prods[prob][g, c, 1 - l] + cores[prob][g, 1 - l]
        to_twin(prob, g).start()

    def finish(prob, st, gl):
        g = st * 2 + gl
        to_twin(prob, g).wait_recv()
        value = prods[prob][g, c, l] + cores[prob][g, l] + lasts[prob][g]
        if prob == 1:
            rows = at(g * SUB, SUB)
            out[1, rows, :] = 0.95 * old[1, rows, :] + 0.05 * value
            out_copy(1, g).start()
        else:
            total[at(g * 64, 64), :] = value

            @pl.when(gl == 1)
            def _():
                cols = slice(st * 128, (st + 1) * 128)
                for n in range(4):
                    rows = slice(n * 256, (n + 1) * 256)
                    out[0, rows, cols] = 0.95 * old[0, rows, cols] + 0.05 * total[cols, rows].T
                out_copy(0, st).start()

    def pass_on(i, n, src):
        dst = rec.at[i // 2, at((i % 2) * 512 + n * CHUNK, CHUNK)]
        return pltpu.make_async_remote_copy(
            src_ref=dst if src is None else src, dst_ref=dst, send_sem=bc_send.at[i], recv_sem=bc_recv.at[i, n],
            device_id=onward[i], device_id_type=MESH)

    @pl.loop(0, STEPS + END + LAG * (RING - 1))
    def _(t):
        for i in range(4):
            prob, st = i // 2, i % 2
            n = t - LAG * away[i]

            @pl.when((n >= 0) & (n < STEPS))
            def _():
                @pl.when(away[i] == 0)
                def _():
                    if prob == 0:
                        g, s, m = st * 2 + n // HALF, (n % HALF) // (HALF // 4), n % (HALF // 4)
                        row = s * SUB + g * 64 + m * CHUNK
                    else:
                        row = st * 512 + n * CHUNK
                    pass_on(i, n, own.at[prob, at(row, CHUNK)]).start()

                @pl.when(away[i] > 0)
                def _():
                    pass_on(i, n, None).wait_recv()

                @pl.when((away[i] > 0) & (away[i] < RING - 1))
                def _():
                    pass_on(i, n, None).start()

        for i in range(4):
            prob, st = i // 2, i % 2
            n = t - LAG * away[i]

            @pl.when((n == HALF - 1) | (n == STEPS - 1))
            def _():
                if st == 0:
                    @pl.when((away[i] == 0) & (n == HALF - 1))
                    def _():
                        pltpu.make_async_copy(own.at[prob], rec.at[prob], own_sem.at[prob]).wait()
                multiply(prob, st * 2 + n // HALF)

            @pl.when((n == HALF - 1 + ADD) | (n == STEPS - 1 + ADD))
            def _():
                add(prob, st * 2 + (n - ADD) // HALF)

            @pl.when((n == HALF - 1 + END) | (n == STEPS - 1 + END))
            def _():
                finish(prob, st, (n - END) // HALF)

    for r in range(4):
        sent = own.at[r // 2, pl.ds(0, 14 * SUB * SUB // DEPTH)]
        pltpu.make_async_copy(sent, sent, ag_send.at[r]).wait()
    for i in range(4):
        @pl.when(away[i] < RING - 1)
        def _():
            sent = rec.at[i // 2, pl.ds(0, 512)]
            pltpu.make_async_copy(sent, sent, bc_send.at[i]).wait()

    @pl.when(h == 1)
    def _():
        for u in range(4):
            swap(u).wait_send()
    for dl, dc in ((1, 0), (1, 1), (0, 1)):
        mix(dl, dc).wait_send()
    for prob in range(2):
        for g in range(4):
            to_mate(prob, g).wait_send()
            to_twin(prob, g).wait_send()
    for prob in range(2):
        for n in range(2 + 2 * prob):
            out_copy(prob, n).wait()


def on_device(gradient, left_old, right_old):
    factor = jax.ShapeDtypeStruct((ROW, SUB), F32)
    anywhere = pl.BlockSpec(memory_space=pl.ANY)
    dma = pltpu.SemaphoreType.DMA
    return pl.pallas_call(
        kernel,
        out_shape=(factor, factor),
        in_specs=[anywhere] * 3,
        out_specs=(anywhere, anywhere),
        scratch_shapes=[
            pltpu.VMEM((ROW, SUB), BF16), pltpu.VMEM((SUB, ROW), BF16),
            pltpu.VMEM((2, ROW, DEPTH), BF16), pltpu.VMEM((2, ROW, DEPTH), BF16),
            pltpu.VMEM((4, 2, 2, 64, ROW), F32), pltpu.VMEM((4, 2, 2, SUB, SUB), F32),
            pltpu.VMEM((4, 2, 64, ROW), F32), pltpu.VMEM((4, 2, SUB, SUB), F32),
            pltpu.VMEM((4, 64, ROW), F32), pltpu.VMEM((4, SUB, SUB), F32),
            pltpu.VMEM((4, 64, ROW), F32), pltpu.VMEM((4, SUB, SUB), F32),
            pltpu.VMEM((SUB, ROW), F32), pltpu.VMEM((2, ROW, SUB), F32), pltpu.VMEM((2, ROW, SUB), F32),
            dma((3,)), dma((4,)), dma((4,)), dma((4,)), dma((4,)), dma((4,)), dma((4, 14)), dma((4,)), dma((4, STEPS)),
            dma((2,)), dma((2, 4)), dma((2, 4)), dma((2, 4)), dma((2, 4)), dma((2, 4)),
        ],
        compiler_params=pltpu.CompilerParams(collective_id=0, has_side_effects=True, vmem_limit_bytes=56 << 20),
        cost_estimate=pl.CostEstimate(flops=4 * ROW * SUB * 8192, bytes_accessed=5 << 20, transcendentals=0),
        name="gram_factors",
    )(gradient, left_old, right_old)


def solution(mesh):
    placed = (P("row", "col"), P("row", "col"), P("row", "col"))
    return jax.shard_map(
        on_device,
        mesh=mesh,
        in_specs=placed,
        out_specs=(P("row", "col"), P("row", "col")),
        check_vma=False,
    )
```

time: 463 us -> 175 us (0.38)
  the two profiles are of different devices: /device:TPU:16 before, /device:TPU:34 now
where the time goes in v1:
time: 175 us
  Pallas kernels  171 us (98%)
  local copies, waits for them, and re-layouts  3.32 us (2%)
    pallas_call x1, Pallas kernels, on_device(): pl.pallas_call(kernel, out_shape=(factor, factor), in_specs=[anywhere] *...  171 us

profile of v1, /device:TPU:34, one launch (start us, length us, event | category | flops | bytes accessed | tf_op | source)
XLA Modules:
  0.0 175.2 jit_solution(15115857554903987407)
XLA Ops:
  0.6 171.3 %gram_factors.1 = (f32[1024,256]{1,0:T(8,128)}, f32[1024,256]{1,0:T(8,128)}) custom-call(bf16[1024,256]{1,0:T(8,128)(2,1)} %g_ref.1, f32[1024,256]{1,0:T(8,128)} %lo_ref.1, f32[1024,256]{1,0:T(8,128)} %ro_ref.1), custom_call_target="tpu_custom_call" | custom-call | flops 8589934592 | bytes 5242880 | tf_op jit(solution)/shard_map/gram_factors/pallas_call | solution.py:285
  171.9 0.0 copy-start
  171.9 2.4 %copy.7 = f32[1024,256]{1,0:T(8,128)} copy(f32[1024,256]{1,0:T(8,128)} %get-tuple-element.4) | data formatting | bytes 2097152
  174.3 0.0 copy-done
  174.3 1.0 copy.8
Async XLA Ops:
  171.9 2.4 %copy-start = (f32[1024,256]{1,0:T(8,128)S(1)}, f32[1024,256]{1,0:T(8,128)}, u32[]{:S(2)}) copy-start(f32[1024,256]{1,0:T(8,128)} %get-tuple-element.5) | copy-start | bytes 3145732

commit v2 on v0

v2 whole, which is shorter than its diff:
```python
import jax
import jax.numpy as jnp
from jax import lax
from jax.experimental import pallas as pl
from jax.experimental.pallas import tpu as pltpu
from jax.sharding import PartitionSpec as P

MESH = pl.DeviceIdType.MESH
BF16, F32 = jnp.bfloat16, jnp.float32
ROW = 1024
SUB = 256
RING = 8
DEPTH = RING * SUB
CHUNK = 16
COUNT = (22, 21, 21)
LAG = 3
ADD, END = 6, 12
READY = (5, 10, 15, 21)
LEVEL = ((0, 3, 1, 2, 2, 3, 3, 4), (0, 3, 3, 4, 2, 3, 1, 2), (0, 1, 3, 2, 4, 3, 3, 2))
ONWARD = (((0, 2, 4, 5), (3,), (2, 4)), ((7,), (0, 6, 4, 7, 5), (6,)), ((1, 3), (1,), (0, 3, 7, 5)))
FAR, HERE = 3, 4


def at(start, size):
    return pl.ds(pl.multiple_of(start, size), size)


def one_of(value, choices):
    found = value == choices[0]
    for choice in choices[1:]:
        found = found | (value == choice)
    return found


def lookup(index, values):
    result = jnp.int32(0)
    for place, value in enumerate(values):
        result = result + jnp.where(index == place, value, 0)
    return result


def kernel(g_ref, lo_ref, ro_ref, l_ref, r_ref,
           grad, turned, own, rec, prod_l, core_l, chip_l, last_l, total, prod_r, core_r, chip_r, last_r, sum_r, stage, old, out,
           load_sem, swap_send, swap_recv, mix_send, mix_recv, line_send, line_recv, x_send, x_recv, y_send, y_recv,
           slice_send, slice_recv, tree_send, tree_recv, own_sem,
           lcore_send, lcore_recv, lchip_send, lchip_recv, rcore_send, rcore_recv, rchip_send, rchip_recv,
           home_send, home_recv, out_sem):
    a, j = lax.axis_index("row"), lax.axis_index("col")
    y, h = a // 2, a % 2
    z, l, c = j // 4, (j // 2) % 2, j % 2
    mine = l * 2 + c

    def line(step):
        return (a, ((z + step + RING) % RING) * 4 + mine)

    def along_y(step):
        return (((y + step + 4) % 4) * 2 + h, j)

    def inside(dl, dc):
        return (a, z * 4 + ((l + dl) % 2) * 2 + (c + dc) % 2)

    def in_plane(row):
        return (row, z * 4 + ((l + h + row) % 2) * 2 + c)

    lines = (line(1), line(-1))
    mate, twin = inside(0, 1), inside(1, 0)
    across = (y * 2 + 1 - h, z * 4 + (1 - l) * 2 + c)
    plane = (along_y(1), along_y(-1), across)

    grad_in = pltpu.make_async_copy(g_ref, grad, load_sem.at[0])
    grad_in.start()
    old_in = [pltpu.make_async_copy(ref, old.at[q], load_sem.at[1 + q]) for q, ref in enumerate((lo_ref, ro_ref))]
    for copy in old_in:
        copy.start()

    def kept(u):
        rows = pl.ds(u * 512, 512)
        return pltpu.make_async_copy(
            g_ref.at[rows, at(h * 128, 128)], own.at[0, rows, at(z * SUB + h * 128, 128)], swap_recv.at[u])

    def swap(u):
        rows = pl.ds(u * 512, 512)
        return pltpu.make_async_remote_copy(
            src_ref=g_ref.at[rows, at((1 - h) * 128, 128)], dst_ref=own.at[0, rows, at(z * SUB + (1 - h) * 128, 128)],
            send_sem=swap_send.at[u], recv_sem=swap_recv.at[2 + u], device_id=twin, device_id_type=MESH)

    kept(0).start()
    kept(1).start()

    barrier = pltpu.get_barrier_semaphore()
    for device in lines + (mate, twin, inside(1, 1)):
        pl.semaphore_signal(barrier, inc=1, device_id=device, device_id_type=MESH)
    for step in range(1, RING):
        pl.semaphore_signal(barrier, inc=1, device_id=in_plane((a + step) % RING), device_id_type=MESH)
    pl.semaphore_wait(barrier, 12)

    swap(0).start()
    swap(1).start()

    def gather(r, q):
        step, u = q // 4, q % 4
        if r == 1:
            u = u + jnp.where(step == 3, 2, 0)
        k = (z - (1 - 2 * r) * step + RING) % RING
        side = jnp.where(u < 2, h, 1 - h)
        part = own.at[0, at((u % 2) * 512, 512), at(k * SUB + side * 128, 128)]
        return pltpu.make_async_remote_copy(
            src_ref=part, dst_ref=part, send_sem=line_send.at[r], recv_sem=line_recv.at[r, q],
            device_id=lines[r], device_id_type=MESH)

    for u in range(2):
        kept(u).wait()
        gather(0, u).start()
        gather(1, u).start()

    grad_in.wait()
    for u in range(4):
        turned[:, u * SUB:(u + 1) * SUB] = grad[u * SUB:(u + 1) * SUB, :].T

    def mix(dl, dc):
        part = ((l + dl + h) % 2) * 2 + (c + dc) % 2
        src = turned.at[:, at(part * SUB, SUB)]
        dst = own.at[1, at(mine * SUB, SUB), at(a * SUB, SUB)]
        if dl == dc == 0:
            return pltpu.make_async_copy(src, dst, mix_recv.at[mine])
        return pltpu.make_async_remote_copy(
            src_ref=src, dst_ref=dst, send_sem=mix_send.at[dl * 2 + dc], recv_sem=mix_recv.at[mine],
            device_id=inside(dl, dc), device_id_type=MESH)

    for dl, dc in ((1, 0), (1, 1), (0, 1), (0, 0)):
        mix(dl, dc).start()

    def in_y(r, n):
        late = n >= 8
        kind = jnp.where(late, (n - 8) // 2, n // 4)
        v = jnp.where(late, (n - 8) % 2 + 2 * r, n % 4)
        from_y = (y - jnp.where(late, 1 - 2 * r, 0) + 4) % 4
        k = from_y * 2 + (h + kind) % 2
        u = (v + 2 * ((l + kind) % 2)) % 4
        part = own.at[1, at(u * SUB, SUB), at(k * SUB, SUB)]
        return pltpu.make_async_remote_copy(
            src_ref=part, dst_ref=part, send_sem=y_send.at[r], recv_sem=y_recv.at[r, n],
            device_id=plane[r], device_id_type=MESH)

    def over_x(u):
        part = own.at[1, at(u * SUB, SUB), at(a * SUB, SUB)]
        return pltpu.make_async_remote_copy(
            src_ref=part, dst_ref=part, send_sem=x_send.at[0], recv_sem=x_recv.at[u], device_id=across, device_id_type=MESH)

    for u in range(2):
        swap(u).wait_recv()
        gather(0, 2 + u).start()
        gather(1, 2 + u).start()
    for v in range(4):
        u = (v + 2 * l) % 4
        here = own.at[1, at(u * SUB, SUB), at(a * SUB, SUB)]
        pltpu.make_async_copy(here, here, mix_recv.at[u]).wait()
        over_x(u).start()
        in_y(0, v).start()
        in_y(1, v).start()

    @pl.loop(4, 14)
    def _(q):
        gather(0, q - 4).wait_recv()
        gather(0, q).start()
        gather(1, q - jnp.where(q < 12, 4, 2)).wait_recv()
        gather(1, q).start()

        @pl.when(q < 8)
        def _():
            over_x((q + 2 * (1 - l)) % 4).wait_recv()

        for r in range(2):
            @pl.when((q >= 8) & (q < 12))
            def _():
                in_y(r, (q - 8) % 2 + jnp.where(q < 10, 0, 4) + 2 * r).wait_recv()

            @pl.when(q < 12)
            def _():
                in_y(r, q).start()

    for r in range(2):
        for n in (2 - 2 * r, 3 - 2 * r, 6 - 2 * r, 7 - 2 * r, 8, 9, 10, 11):
            in_y(r, n).wait_recv()

    def slices(r, q):
        step, u = q // 4, (q + 2 * r) % 4

        def slot(steps):
            return jnp.where(steps == 4, 768, (steps - 1) * SUB + r * 128)

        dst = rec.at[1, at(slot(step + 1) + u * 32, 32)]

        def copy(src):
            return pltpu.make_async_remote_copy(
                src_ref=src, dst_ref=dst, send_sem=slice_send.at[r], recv_sem=slice_recv.at[r, q],
                device_id=lines[r], device_id_type=MESH)

        return copy(own.at[1, at(a * 128 + u * 32, 32)]), copy(rec.at[1, at(slot(jnp.maximum(step, 1)) + u * 32, 32)])

    for q in range(4):
        for r in range(2):
            slices(r, q)[0].start()

    for q in range(10, 14):
        gather(0, q).wait_recv()
        gather(1, q if q >= 12 else q - 2).wait_recv()

    for copy in old_in:
        copy.wait()

    node = ((y - z // 2 + 4) % 4) * 2 + (h + z % 2) % 2
    root = node == 0
    level = [lookup(node, LEVEL[tree]) for tree in range(3)]
    deepest = jnp.maximum(jnp.maximum(level[0], level[1]), level[2])

    def source_row(place):
        return ((place % 16) // 4) * SUB + (place // 16) * 64 + (place % 4) * CHUNK

    @pl.when(root)
    def _():
        @pl.loop(0, 16)
        def _(n):
            pltpu.make_async_copy(
                own.at[0, at((n % 4) * SUB + (n // 4) * 64, 64)], rec.at[0, at(n * 64, 64)], own_sem.at[0]).start()

    def pass_on(tree, n, way, first):
        place = 3 * n + tree
        dst = rec.at[0, at(place * CHUNK, CHUNK)]
        src = own.at[0, at(source_row(place), CHUNK)] if first else dst
        return pltpu.make_async_remote_copy(
            src_ref=src, dst_ref=dst, send_sem=tree_send.at[tree, way], recv_sem=tree_recv.at[tree, n],
            device_id=plane[way], device_id_type=MESH)

    def l_mate(g):
        return pltpu.make_async_remote_copy(
            src_ref=prod_l.at[g, 1 - c], dst_ref=core_l.at[g],
            send_sem=lcore_send.at[g], recv_sem=lcore_recv.at[g], device_id=mate, device_id_type=MESH)

    def l_twin(g):
        return pltpu.make_async_remote_copy(
            src_ref=chip_l.at[g], dst_ref=last_l.at[g],
            send_sem=lchip_send.at[g], recv_sem=lchip_recv.at[g], device_id=twin, device_id_type=MESH)

    def l_out(half):
        cols = pl.ds(half * 128, 128)
        return pltpu.make_async_copy(out.at[0, :, cols], l_ref.at[:, cols], out_sem.at[0, half])

    def l_multiply(g, n):
        tile = lax.dot_general(
            rec[0, at(g * SUB, SUB), :], own[0, at(n * SUB, SUB), :],
            (((1,), (1,)), ((), ())), preferred_element_type=F32)
        for s in range(4):
            prod_l[g, s % 2, s // 2, :, at(n * SUB, SUB)] = tile[s * 64:(s + 1) * 64, :]

        @pl.when(n == 3)
        def _():
            l_mate(g).start()

    def l_add(g):
        l_mate(g).wait_recv()
        chip_l[g] = prod_l[g, c, 1 - l] + core_l[g, 1 - l]
        l_twin(g).start()

    def l_finish(g):
        l_twin(g).wait_recv()
        total[at(g * 64, 64), :] = prod_l[g, c, l] + core_l[g, l] + last_l[g]
        for half in range(2):
            @pl.when(g == 2 * half + 1)
            def _():
                cols = slice(half * 128, (half + 1) * 128)
                for n in range(4):
                    rows = slice(n * 256, (n + 1) * 256)
                    out[0, rows, cols] = 0.95 * old[0, rows, cols] + 0.05 * total[cols, rows].T
                l_out(half).start()

    def r_mate(g, size):
        rows = pl.ds(0, size)
        return pltpu.make_async_remote_copy(
            src_ref=prod_r.at[g, 1 - c, :, rows], dst_ref=core_r.at[g, :, rows],
            send_sem=rcore_send.at[g], recv_sem=rcore_recv.at[g], device_id=mate, device_id_type=MESH)

    def r_twin(g, size):
        rows = pl.ds(0, size)
        return pltpu.make_async_remote_copy(
            src_ref=chip_r.at[g, rows], dst_ref=last_r.at[g, rows],
            send_sem=rchip_send.at[g], recv_sem=rchip_recv.at[g], device_id=twin, device_id_type=MESH)

    def r_multiply(g, size, operand, step):
        s_c, s_l = (1 - c + step // 2) % 2, step % 2
        prod_r[g, s_c, s_l, 0:size] = lax.dot_general(
            operand[...], own[1, at((s_l * 2 + s_c) * SUB, SUB), :],
            (((1,), (1,)), ((), ())), preferred_element_type=F32)

        @pl.when(step == 1)
        def _():
            r_mate(g, size).start()

    def kept_l(g):
        return (l + h + z + (jnp.where(g < FAR, g + 1, 0) if not isinstance(g, int) else 0)) % 2

    def r_add(g, size):
        r_mate(g, size).wait_recv()
        chip_r[g, 0:size] = prod_r[g, c, 1 - kept_l(g), 0:size] + core_r[g, 1 - kept_l(g), 0:size]
        r_twin(g, size).start()

    def home(g, part):
        if isinstance(g, int):
            b = (z + (4 if g == FAR else 0)) % RING
        else:
            b = (z + (2 * part - 1) * (g + 1) + RING) % RING
        src, dst = sum_r.at[g, pl.ds(part * 128, 128)], stage.at[a]
        here = pltpu.make_async_copy(src, dst, home_recv.at[a])
        away = pltpu.make_async_remote_copy(
            src_ref=src, dst_ref=dst, send_sem=home_send.at[g, part], recv_sem=home_recv.at[a],
            device_id=in_plane(b), device_id_type=MESH)
        return b, here, away

    def r_finish(g, size):
        r_twin(g, size).wait_recv()
        sum_r[g, 0:size] = prod_r[g, c, kept_l(g), 0:size] + core_r[g, kept_l(g), 0:size] + last_r[g, 0:size]
        for part in range(size // 128):
            b, here, away = home(g, part)

            @pl.when(b == a)
            def _():
                here.start()

            @pl.when(b != a)
            def _():
                away.start()

    def r_out(n):
        rows = pl.ds(n * 128, 128)
        return pltpu.make_async_copy(out.at[1, rows], r_ref.at[rows], out_sem.at[1, n])

    @pl.loop(0, 47)
    def _(t):
        for tree in range(3):
            n = t - LAG * level[tree]

            @pl.when((n >= 0) & (n < COUNT[tree]))
            def _():
                @pl.when(root)
                def _():
                    pass_on(tree, n, tree, True).start()

                @pl.when(node > 0)
                def _():
                    pass_on(tree, n, 0, False).wait_recv()

                for way in range(3):
                    senders = tuple(v for v in ONWARD[tree][way] if v > 0)
                    if senders:
                        @pl.when(one_of(node, senders))
                        def _():
                            pass_on(tree, n, way, False).start()

        q = t // 2

        @pl.when(t % 2 == 0)
        def _():
            @pl.when((q >= 4) & (q < 18))
            def _():
                for r in range(2):
                    slices(r, q - 4)[0].wait_recv()

                    @pl.when(q < 14)
                    def _():
                        slices(r, q)[1].start()

        n = t - LAG * deepest

        @pl.when(root & (t == READY[0]))
        def _():
            pltpu.make_async_copy(own.at[0], rec.at[0], own_sem.at[0]).wait()

        for ready in READY:
            @pl.when((n >= ready) & (n < ready + 4))
            def _():
                l_multiply(READY.index(ready), n - ready)

        @pl.when(one_of(n - ADD, READY))
        def _():
            l_add((n - ADD) // 5 - 1)

        @pl.when(one_of(n - END, READY))
        def _():
            l_finish((n - END) // 5 - 1)

        @pl.when((t >= 2) & (t < 6))
        def _():
            r_multiply(HERE, 128, own.at[1, at(a * 128, 128)], t - 2)

        @pl.when(t == 6)
        def _():
            r_add(HERE, 128)

        @pl.when(t == 11)
        def _():
            r_finish(HERE, 128)

        m = t - 15

        @pl.when((m >= 0) & (m < 24) & (m % 8 < 4))
        def _():
            g = m // 8
            r_multiply(g, 256, rec.at[1, at(g * SUB, SUB)], m % 8)

        @pl.when((m >= 0) & (m < 24) & (m % 8 == 4))
        def _():
            r_add(m // 8, 256)

        @pl.when((m >= 9) & (m < 32) & (m % 8 == 1))
        def _():
            r_finish(m // 8 - 1, 256)

        @pl.when(t == 36)
        def _():
            @pl.loop(0, 4)
            def _(step):
                r_multiply(FAR, 128, rec.at[1, pl.ds(768, 128)], step)

        @pl.when(t == 37)
        def _():
            r_add(FAR, 128)

        @pl.when(t == 41)
        def _():
            r_finish(FAR, 128)

    for n in range(RING):
        rows = slice(n * 128, (n + 1) * 128)
        pltpu.make_async_copy(stage.at[n], stage.at[n], home_recv.at[n]).wait()
        out[1, rows, :] = 0.95 * old[1, rows, :] + 0.05 * stage[n]
        r_out(n).start()

    def sent(ref, sem):
        pltpu.make_async_copy(ref, ref, sem).wait()

    for r in range(2):
        sent(own.at[0, pl.ds(0, 448)], line_send.at[r])
        sent(own.at[1, pl.ds(0, 384)], y_send.at[r])
        sent(own.at[1, pl.ds(0, 448)], slice_send.at[r])
    sent(own.at[1, pl.ds(0, 128)], x_send.at[0])
    for tree in range(3):
        for way in range(3):
            if ONWARD[tree][way]:
                @pl.when(one_of(node, ONWARD[tree][way]))
                def _():
                    sent(rec.at[0, pl.ds(0, COUNT[tree] * CHUNK)], tree_send.at[tree, way])
    for u in range(2):
        swap(u).wait_send()
    for dl, dc in ((1, 0), (1, 1), (0, 1)):
        mix(dl, dc).wait_send()
    for g in range(4):
        l_mate(g).wait_send()
        l_twin(g).wait_send()
    for g in range(5):
        size = 256 if g < 3 else 128
        r_mate(g, size).wait_send()
        r_twin(g, size).wait_send()
        for part in range(size // 128):
            b, here, away = home(jnp.int32(g) if g < 3 else g, part)

            @pl.when(b != a)
            def _():
                away.wait_send()
    for half in range(2):
        l_out(half).wait()
    for n in range(RING):
        r_out(n).wait()


def on_device(gradient, left_old, right_old):
    factor = jax.ShapeDtypeStruct((ROW, SUB), F32)
    anywhere = pl.BlockSpec(memory_space=pl.ANY)
    dma = pltpu.SemaphoreType.DMA
    return pl.pallas_call(
        kernel,
        out_shape=(factor, factor),
        in_specs=[anywhere] * 3,
        out_specs=(anywhere, anywhere),
        scratch_shapes=[
            pltpu.VMEM((ROW, SUB), BF16), pltpu.VMEM((SUB, ROW), BF16),
            pltpu.VMEM((2, ROW, DEPTH), BF16), pltpu.VMEM((2, ROW, DEPTH), BF16),
            pltpu.VMEM((4, 2, 2, 64, ROW), F32), pltpu.VMEM((4, 2, 64, ROW), F32), pltpu.VMEM((4, 64, ROW), F32),
            pltpu.VMEM((4, 64, ROW), F32), pltpu.VMEM((SUB, ROW), F32),
            pltpu.VMEM((5, 2, 2, SUB, SUB), F32), pltpu.VMEM((5, 2, SUB, SUB), F32), pltpu.VMEM((5, SUB, SUB), F32),
            pltpu.VMEM((5, SUB, SUB), F32), pltpu.VMEM((5, SUB, SUB), F32), pltpu.VMEM((RING, 128, SUB), F32),
            pltpu.VMEM((2, ROW, SUB), F32), pltpu.VMEM((2, ROW, SUB), F32),
            dma((3,)), dma((2,)), dma((4,)), dma((4,)), dma((4,)), dma((2,)), dma((2, 14)), dma((1,)), dma((4,)), dma((2,)),
            dma((2, 12)), dma((2,)), dma((2, 14)), dma((3, 3)), dma((3, 22)), dma((1,)),
            dma((4,)), dma((4,)), dma((4,)), dma((4,)), dma((5,)), dma((5,)), dma((5,)), dma((5,)),
            dma((5, 2)), dma((RING,)), dma((2, RING)),
        ],
        compiler_params=pltpu.CompilerParams(collective_id=0, has_side_effects=True, vmem_limit_bytes=56 << 20),
        cost_estimate=pl.CostEstimate(flops=4 * ROW * SUB * 8192, bytes_accessed=5 << 20, transcendentals=0),
        name="gram_factors",
    )(gradient, left_old, right_old)


def solution(mesh):
    placed = (P("row", "col"), P("row", "col"), P("row", "col"))
    return jax.shard_map(
        on_device,
        mesh=mesh,
        in_specs=placed,
        out_specs=(P("row", "col"), P("row", "col")),
        check_vma=False,
    )
```

time: 463 us -> 142 us (0.31)
  waiting for transfers between devices: 414 us -> 0 us
  Pallas kernels: 0 us -> 138 us
  matrix products: 22.1 us -> 0 us
  between operations: 13.8 us -> 0.65 us
  other arithmetic: 6.38 us -> 0 us
    psum x1 -> x0, waiting for transfers between devices: 173 us -> none  [broadcast(): return lax.psum(block, axis)]
    pallas_call x0 -> x1, Pallas kernels: none -> 138 us  [on_device(): pl.pallas_call(kernel, out_shape=(factor, factor), in_specs=[anywhere] *...]
    all_gather x1 -> x0, waiting for transfers between devices: 129 us -> none  [on_device(): panel = lax.all_gather(gradient, 'col', axis=1, tiled=True)]
    reduce_scatter x1 -> x0, waiting for transfers between devices: 112 us -> none  [on_device(): lax.psum_scatter(lax.dot_general(panel, gradient, (((0,), (0,)), ((), ())...]
    dot_general x2 -> x0, matrix products: 22.1 us -> none  [the longest x1 12.7 us: on_device(): lax.dot_general(panel, gradient, (((0,), (0,)), ((), ())), preferred_elem...]
    select_n x1 -> x0, other arithmetic: 4.95 us -> none  [broadcast(): jnp.where(lax.axis_index(axis) == owner, block, jnp.zeros_like(block))]
  transfers between devices with their start and end apart: 3 -> 0, of which waited for: 3 -> 0; matrix products, arithmetic and copies ran while one was open for 5% -> 0% of each run, Pallas kernels for 0% -> 0%
where the time goes in v2:
time: 142 us
  Pallas kernels  138 us (97%)
  local copies, waits for them, and re-layouts  3.32 us (2%)
    pallas_call x1, Pallas kernels, on_device(): pl.pallas_call(kernel, out_shape=(factor, factor), in_specs=[anywhere] *...  138 us
    unnamed x4, local copies, waits for them, and re-layouts  3.32 us

profile of v2, /device:TPU:16, one launch (start us, length us, event | category | flops | bytes accessed | tf_op | source)
XLA Modules:
  0.0 141.8 jit_solution(18399447965336804067)
XLA Ops:
  0.6 137.8 %gram_factors.1 = (f32[1024,256]{1,0:T(8,128)}, f32[1024,256]{1,0:T(8,128)}) custom-call(bf16[1024,256]{1,0:T(8,128)(2,1)} %g_ref.1, f32[1024,256]{1,0:T(8,128)} %lo_ref.1, f32[1024,256]{1,0:T(8,128)} %ro_ref.1), custom_call_target="tpu_custom_call" | custom-call | flops 8589934592 | bytes 5242880 | tf_op jit(solution)/shard_map/gram_factors/pallas_call | solution.py:479
  138.4 0.0 copy-start
  138.5 2.4 %copy.7 = f32[1024,256]{1,0:T(8,128)} copy(f32[1024,256]{1,0:T(8,128)} %get-tuple-element.4) | data formatting | bytes 2097152
  140.8 0.0 copy-done
  140.8 1.0 copy.8
Async XLA Ops:
  138.4 2.4 %copy-start = (f32[1024,256]{1,0:T(8,128)S(1)}, f32[1024,256]{1,0:T(8,128)}, u32[]{:S(2)}) copy-start(f32[1024,256]{1,0:T(8,128)} %get-tuple-element.5) | copy-start | bytes 3145732

commit v3 on v2

--- a/solution.py
+++ b/solution.py
@@ -13,12 +13,15 @@
 DEPTH = RING * SUB
 CHUNK = 16
 COUNT = (22, 21, 21)
-LAG = 3
-ADD, END = 6, 12
+HOME = 23
+START = 0
+LAG = 4
+ADD, END = 4, 9
 READY = (5, 10, 15, 21)
 LEVEL = ((0, 3, 1, 2, 2, 3, 3, 4), (0, 3, 3, 4, 2, 3, 1, 2), (0, 1, 3, 2, 4, 3, 3, 2))
 ONWARD = (((0, 2, 4, 5), (3,), (2, 4)), ((7,), (0, 6, 4, 7, 5), (6,)), ((1, 3), (1,), (0, 3, 7, 5)))
-FAR, HERE = 3, 4
+FAR, HERE = 3, 5
+SIZES, PARTS = (256, 256, 256, 64, 64, 128), (2, 2, 2, 2, 2, 1)
 
 
 def at(start, size):
@@ -39,8 +42,8 @@
     return result
 
 
-def kernel(g_ref, lo_ref, ro_ref, l_ref, r_ref,
-           grad, turned, own, rec, prod_l, core_l, chip_l, last_l, total, prod_r, core_r, chip_r, last_r, sum_r, stage, old, out,
+def kernel(g_ref, l_ref, r_ref,
+           grad, turned, own, rec, prod_l, core_l, chip_l, last_l, total, prod_r, core_r, chip_r, last_r, sum_r, out,
            load_sem, swap_send, swap_recv, mix_send, mix_recv, line_send, line_recv, x_send, x_recv, y_send, y_recv,
            slice_send, slice_recv, tree_send, tree_recv, own_sem,
            lcore_send, lcore_recv, lchip_send, lchip_recv, rcore_send, rcore_recv, rchip_send, rchip_recv,
@@ -69,9 +72,6 @@
 
     grad_in = pltpu.make_async_copy(g_ref, grad, load_sem.at[0])
     grad_in.start()
-    old_in = [pltpu.make_async_copy(ref, old.at[q], load_sem.at[1 + q]) for q, ref in enumerate((lo_ref, ro_ref))]
-    for copy in old_in:
-        copy.start()
 
     def kept(u):
         rows = pl.ds(u * 512, 512)
@@ -187,16 +187,16 @@
         step, u = q // 4, (q + 2 * r) % 4
 
         def slot(steps):
-            return jnp.where(steps == 4, 768, (steps - 1) * SUB + r * 128)
-
-        dst = rec.at[1, at(slot(step + 1) + u * 32, 32)]
+            return (steps - 1) * SUB + r * 128 + u * 32
+
+        dst = rec.at[1, at(jnp.where(step == 3, 768 + (q % 4) * 64 + r * 32, slot(step + 1)), 32)]
 
         def copy(src):
             return pltpu.make_async_remote_copy(
                 src_ref=src, dst_ref=dst, send_sem=slice_send.at[r], recv_sem=slice_recv.at[r, q],
                 device_id=lines[r], device_id_type=MESH)
 
-        return copy(own.at[1, at(a * 128 + u * 32, 32)]), copy(rec.at[1, at(slot(jnp.maximum(step, 1)) + u * 32, 32)])
+        return copy(own.at[1, at(a * 128 + u * 32, 32)]), copy(rec.at[1, at(slot(jnp.maximum(step, 1)), 32)])
 
     for q in range(4):
         for r in range(2):
@@ -205,9 +205,6 @@
     for q in range(10, 14):
         gather(0, q).wait_recv()
         gather(1, q if q >= 12 else q - 2).wait_recv()
-
-    for copy in old_in:
-        copy.wait()
 
     node = ((y - z // 2 + 4) % 4) * 2 + (h + z % 2) % 2
     root = node == 0
@@ -244,16 +241,16 @@
 
     def l_out(half):
         cols = pl.ds(half * 128, 128)
-        return pltpu.make_async_copy(out.at[0, :, cols], l_ref.at[:, cols], out_sem.at[0, half])
+        return pltpu.make_async_copy(out.at[:, cols], l_ref.at[:, cols], out_sem.at[half])
 
     def l_multiply(g, n):
         tile = lax.dot_general(
-            rec[0, at(g * SUB, SUB), :], own[0, at(n * SUB, SUB), :],
+            rec[0, at(g * SUB, SUB), :], own[0, at(n * 512, 512), :],
             (((1,), (1,)), ((), ())), preferred_element_type=F32)
         for s in range(4):
-            prod_l[g, s % 2, s // 2, :, at(n * SUB, SUB)] = tile[s * 64:(s + 1) * 64, :]
-
-        @pl.when(n == 3)
+            prod_l[g, s % 2, s // 2, :, at(n * 512, 512)] = tile[s * 64:(s + 1) * 64, :]
+
+        @pl.when(n == 1)
         def _():
             l_mate(g).start()
 
@@ -271,7 +268,7 @@
                 cols = slice(half * 128, (half + 1) * 128)
                 for n in range(4):
                     rows = slice(n * 256, (n + 1) * 256)
-                    out[0, rows, cols] = 0.95 * old[0, rows, cols] + 0.05 * total[cols, rows].T
+                    out[rows, cols] = total[cols, rows].T
                 l_out(half).start()
 
     def r_mate(g, size):
@@ -286,15 +283,21 @@
             src_ref=chip_r.at[g, rows], dst_ref=last_r.at[g, rows],
             send_sem=rchip_send.at[g], recv_sem=rchip_recv.at[g], device_id=twin, device_id_type=MESH)
 
-    def r_multiply(g, size, operand, step):
-        s_c, s_l = (1 - c + step // 2) % 2, step % 2
-        prod_r[g, s_c, s_l, 0:size] = lax.dot_general(
-            operand[...], own[1, at((s_l * 2 + s_c) * SUB, SUB), :],
-            (((1,), (1,)), ((), ())), preferred_element_type=F32)
-
-        @pl.when(step == 1)
-        def _():
-            r_mate(g, size).start()
+    def r_multiply(g, operand, n):
+        tile = lax.dot_general(
+            operand[...], own[1, at(n * 512, 512), :], (((1,), (1,)), ((), ())), preferred_element_type=F32)
+        for core in range(2):
+            prod_r[g, core, n] = tile[:, core * SUB:(core + 1) * SUB]
+
+        @pl.when(n == 1)
+        def _():
+            r_mate(g, 256).start()
+
+    def r_multiply_few(g, size, operand):
+        tile = lax.dot_general(operand[...], own[1], (((1,), (1,)), ((), ())), preferred_element_type=F32)
+        for s in range(4):
+            prod_r[g, s % 2, s // 2, 0:size] = tile[:, s * SUB:(s + 1) * SUB]
+        r_mate(g, size).start()
 
     def kept_l(g):
         return (l + h + z + (jnp.where(g < FAR, g + 1, 0) if not isinstance(g, int) else 0)) % 2
@@ -306,38 +309,41 @@
 
     def home(g, part):
         if isinstance(g, int):
-            b = (z + (4 if g == FAR else 0)) % RING
+            b, size = (z + (0 if g == HERE else 4)) % RING, 128 if g == HERE else 32
+            row = a * 128 + (0 if g == HERE else (2 * part + g - FAR) * 32)
         else:
-            b = (z + (2 * part - 1) * (g + 1) + RING) % RING
-        src, dst = sum_r.at[g, pl.ds(part * 128, 128)], stage.at[a]
-        here = pltpu.make_async_copy(src, dst, home_recv.at[a])
-        away = pltpu.make_async_remote_copy(
-            src_ref=src, dst_ref=dst, send_sem=home_send.at[g, part], recv_sem=home_recv.at[a],
-            device_id=in_plane(b), device_id_type=MESH)
-        return b, here, away
-
-    def r_finish(g, size):
+            b, size, row = (z + (2 * part - 1) * (g + 1) + RING) % RING, 128, a * 128
+        src, dst = sum_r.at[g, pl.ds(part * size, size)], r_ref.at[at(row, size)]
+
+        def here():
+            return pltpu.make_async_copy(src, dst, home_recv.at[a])
+
+        def away():
+            return pltpu.make_async_remote_copy(
+                src_ref=src, dst_ref=dst, send_sem=home_send.at[g, part], recv_sem=home_recv.at[a],
+                device_id=in_plane(b), device_id_type=MESH)
+
+        return b == a, here, away
+
+    def r_sum(g, size):
         r_twin(g, size).wait_recv()
         sum_r[g, 0:size] = prod_r[g, c, kept_l(g), 0:size] + core_r[g, kept_l(g), 0:size] + last_r[g, 0:size]
-        for part in range(size // 128):
-            b, here, away = home(g, part)
-
-            @pl.when(b == a)
-            def _():
-                here.start()
-
-            @pl.when(b != a)
-            def _():
-                away.start()
-
-    def r_out(n):
-        rows = pl.ds(n * 128, 128)
-        return pltpu.make_async_copy(out.at[1, rows], r_ref.at[rows], out_sem.at[1, n])
-
-    @pl.loop(0, 47)
+
+    def r_home(g, part):
+        stays, here, away = home(g, part)
+
+        @pl.when(stays)
+        def _():
+            here().start()
+
+        @pl.when(jnp.logical_not(stays))
+        def _():
+            away().start()
+
+    @pl.loop(0, 48)
     def _(t):
         for tree in range(3):
-            n = t - LAG * level[tree]
+            n = t - LAG * level[tree] - START
 
             @pl.when((n >= 0) & (n < COUNT[tree]))
             def _():
@@ -369,14 +375,65 @@
                     def _():
                         slices(r, q)[1].start()
 
-        n = t - LAG * deepest
-
-        @pl.when(root & (t == READY[0]))
+        m = t - 15
+
+        @pl.when((m >= 3) & (m < 24) & (m % 8 == 3))
+        def _():
+            r_add(m // 8, 256)
+
+        for far in range(2):
+            @pl.when(t == 34 + 2 * far)
+            def _():
+                r_add(FAR + far, 64)
+
+        @pl.when((m >= 7) & (m < 31) & (m % 8 == 7))
+        def _():
+            r_sum(m // 8, 256)
+
+        for part in range(2):
+            g = (t - HOME) // 8
+
+            @pl.when((t >= HOME) & (t < HOME + 24) & ((t - HOME) % 8 == 0))
+            def _():
+                r_home(g, part)
+
+        for far in range(2):
+            @pl.when(t == 39 + far)
+            def _():
+                r_sum(FAR + far, 64)
+                r_home(FAR + far, 0)
+                r_home(FAR + far, 1)
+
+        @pl.when((m >= 0) & (m < 24) & (m % 8 < 2))
+        def _():
+            r_multiply(m // 8, rec.at[1, at((m // 8) * SUB, SUB)], m % 8)
+
+        for far in range(2):
+            @pl.when(t == 33 + 2 * far)
+            def _():
+                r_multiply_few(FAR + far, 64, rec.at[1, pl.ds(768 + 64 * far, 64)])
+
+        @pl.when(t == 2)
+        def _():
+            r_multiply_few(HERE, 128, own.at[1, at(a * 128, 128)])
+
+        @pl.when(t == 5)
+        def _():
+            r_add(HERE, 128)
+
+        @pl.when(t == 9)
+        def _():
+            r_sum(HERE, 128)
+            r_home(HERE, 0)
+
+        n = t - LAG * deepest - START
+
+        @pl.when(root & (n == READY[0]))
         def _():
             pltpu.make_async_copy(own.at[0], rec.at[0], own_sem.at[0]).wait()
 
         for ready in READY:
-            @pl.when((n >= ready) & (n < ready + 4))
+            @pl.when((n >= ready) & (n < ready + 2))
             def _():
                 l_multiply(READY.index(ready), n - ready)
 
@@ -388,52 +445,10 @@
         def _():
             l_finish((n - END) // 5 - 1)
 
-        @pl.when((t >= 2) & (t < 6))
-        def _():
-            r_multiply(HERE, 128, own.at[1, at(a * 128, 128)], t - 2)
-
-        @pl.when(t == 6)
-        def _():
-            r_add(HERE, 128)
-
-        @pl.when(t == 11)
-        def _():
-            r_finish(HERE, 128)
-
-        m = t - 15
-
-        @pl.when((m >= 0) & (m < 24) & (m % 8 < 4))
-        def _():
-            g = m // 8
-            r_multiply(g, 256, rec.at[1, at(g * SUB, SUB)], m % 8)
-
-        @pl.when((m >= 0) & (m < 24) & (m % 8 == 4))
-        def _():
-            r_add(m // 8, 256)
-
-        @pl.when((m >= 9) & (m < 32) & (m % 8 == 1))
-        def _():
-            r_finish(m // 8 - 1, 256)
-
-        @pl.when(t == 36)
-        def _():
-            @pl.loop(0, 4)
-            def _(step):
-                r_multiply(FAR, 128, rec.at[1, pl.ds(768, 128)], step)
-
-        @pl.when(t == 37)
-        def _():
-            r_add(FAR, 128)
-
-        @pl.when(t == 41)
-        def _():
-            r_finish(FAR, 128)
 
     for n in range(RING):
-        rows = slice(n * 128, (n + 1) * 128)
-        pltpu.make_async_copy(stage.at[n], stage.at[n], home_recv.at[n]).wait()
-        out[1, rows, :] = 0.95 * old[1, rows, :] + 0.05 * stage[n]
-        r_out(n).start()
+        rows = r_ref.at[pl.ds(n * 128, 128)]
+        pltpu.make_async_copy(rows, rows, home_recv.at[n]).wait()
 
     def sent(ref, sem):
         pltpu.make_async_copy(ref, ref, sem).wait()
@@ -456,48 +471,45 @@
     for g in range(4):
         l_mate(g).wait_send()
         l_twin(g).wait_send()
-    for g in range(5):
-        size = 256 if g < 3 else 128
-        r_mate(g, size).wait_send()
-        r_twin(g, size).wait_send()
-        for part in range(size // 128):
-            b, here, away = home(jnp.int32(g) if g < 3 else g, part)
-
-            @pl.when(b != a)
-            def _():
-                away.wait_send()
+    for g in range(6):
+        r_mate(g, SIZES[g]).wait_send()
+        r_twin(g, SIZES[g]).wait_send()
+        for part in range(PARTS[g]):
+            stays, here, away = home(jnp.int32(g) if g < FAR else g, part)
+
+            @pl.when(jnp.logical_not(stays))
+            def _():
+                away().wait_send()
     for half in range(2):
         l_out(half).wait()
-    for n in range(RING):
-        r_out(n).wait()
 
 
 def on_device(gradient, left_old, right_old):
     factor = jax.ShapeDtypeStruct((ROW, SUB), F32)
     anywhere = pl.BlockSpec(memory_space=pl.ANY)
     dma = pltpu.SemaphoreType.DMA
-    return pl.pallas_call(
+    gram_left, gram_right = pl.pallas_call(
         kernel,
         out_shape=(factor, factor),
-        in_specs=[anywhere] * 3,
+        in_specs=[anywhere],
         out_specs=(anywhere, anywhere),
         scratch_shapes=[
             pltpu.VMEM((ROW, SUB), BF16), pltpu.VMEM((SUB, ROW), BF16),
             pltpu.VMEM((2, ROW, DEPTH), BF16), pltpu.VMEM((2, ROW, DEPTH), BF16),
             pltpu.VMEM((4, 2, 2, 64, ROW), F32), pltpu.VMEM((4, 2, 64, ROW), F32), pltpu.VMEM((4, 64, ROW), F32),
             pltpu.VMEM((4, 64, ROW), F32), pltpu.VMEM((SUB, ROW), F32),
-            pltpu.VMEM((5, 2, 2, SUB, SUB), F32), pltpu.VMEM((5, 2, SUB, SUB), F32), pltpu.VMEM((5, SUB, SUB), F32),
-            pltpu.VMEM((5, SUB, SUB), F32), pltpu.VMEM((5, SUB, SUB), F32), pltpu.VMEM((RING, 128, SUB), F32),
-            pltpu.VMEM((2, ROW, SUB), F32), pltpu.VMEM((2, ROW, SUB), F32),
-            dma((3,)), dma((2,)), dma((4,)), dma((4,)), dma((4,)), dma((2,)), dma((2, 14)), dma((1,)), dma((4,)), dma((2,)),
+            pltpu.VMEM((6, 2, 2, SUB, SUB), F32), pltpu.VMEM((6, 2, SUB, SUB), F32), pltpu.VMEM((6, SUB, SUB), F32),
+            pltpu.VMEM((6, SUB, SUB), F32), pltpu.VMEM((6, SUB, SUB), F32), pltpu.VMEM((ROW, SUB), F32),
+            dma((1,)), dma((2,)), dma((4,)), dma((4,)), dma((4,)), dma((2,)), dma((2, 14)), dma((1,)), dma((4,)), dma((2,)),
             dma((2, 12)), dma((2,)), dma((2, 14)), dma((3, 3)), dma((3, 22)), dma((1,)),
-            dma((4,)), dma((4,)), dma((4,)), dma((4,)), dma((5,)), dma((5,)), dma((5,)), dma((5,)),
-            dma((5, 2)), dma((RING,)), dma((2, RING)),
+            dma((4,)), dma((4,)), dma((4,)), dma((4,)), dma((6,)), dma((6,)), dma((6,)), dma((6,)),
+            dma((6, 2)), dma((RING,)), dma((2,)),
         ],
         compiler_params=pltpu.CompilerParams(collective_id=0, has_side_effects=True, vmem_limit_bytes=56 << 20),
         cost_estimate=pl.CostEstimate(flops=4 * ROW * SUB * 8192, bytes_accessed=5 << 20, transcendentals=0),
         name="gram_factors",
-    )(gradient, left_old, right_old)
+    )(gradient)
+    return 0.95 * left_old + 0.05 * gram_left, 0.95 * right_old + 0.05 * gram_right
 
 
 def solution(mesh):

time: 142 us -> 135 us (0.951); the launches traced: 142 us -> 133 us
  Pallas kernels: 138 us -> 129 us
  local copies, waits for them, and re-layouts: 3.32 us -> 0.01 us
  other arithmetic: 0 us -> 3.2 us
    pallas_call x1, Pallas kernels: 138 us -> 129 us  [on_device(): pl.pallas_call(kernel, out_shape=(factor, factor), in_specs=[anywhere], o...]
    unnamed x4, local copies, waits for them, and re-layouts: 3.32 us -> 0.01 us
    add x0 -> x1, other arithmetic: none -> 3.2 us  [on_device(): 0.95 * right_old + 0.05 * gram_right]
where the time goes in v3:
time: 135 us; the launch traced here: 133 us
  Pallas kernels  129 us (96%)
  other arithmetic  3.2 us (2%)
    pallas_call x1, Pallas kernels, on_device(): pl.pallas_call(kernel, out_shape=(factor, factor), in_specs=[anywhere], o...  129 us
    add x1, other arithmetic, on_device(): 0.95 * right_old + 0.05 * gram_right  3.2 us

profile of v3, /device:TPU:16, one launch (start us, length us, event | category | flops | bytes accessed | tf_op | source)
XLA Modules:
  0.0 132.7 jit_solution(16500151479982100771)
XLA Ops:
  0.6 0.0 copy-start
  0.6 0.0 copy-start.1
  0.6 128.8 %gram_factors.1 = (f32[1024,256]{1,0:T(8,128)}, f32[1024,256]{1,0:T(8,128)}) custom-call(bf16[1024,256]{1,0:T(8,128)(2,1)} %g_ref.1), custom_call_target="tpu_custom_call" | custom-call | flops 8589934592 | bytes 5242880 | tf_op jit(solution)/shard_map/gram_factors/pallas_call | solution.py:491
  129.5 0.0 copy-done
  129.5 0.0 copy-done.1
  129.5 3.2 %multiply_add_fusion = (f32[1024,256]{1,0:T(8,128)}, f32[1024,256]{1,0:T(8,128)}) fusion(f32[1024,256]{1,0:T(8,128)} %get-tuple-element.5, f32[1024,256]{1,0:T(8,128)S(1)} %copy-done, f32[1024,256]{1,0:T(8,128)} %get-tuple-element.4, f32[1024,256]{1,0:T(8,128)S(1)} %copy-done.1), kind=kLoop, calls=%fused_computation | loop fusion | flops 1572864 | bytes 6291456 | tf_op jit(solution)/shard_map/add | solution.py:512
Async XLA Ops:
  0.6 128.8 %copy-start = (f32[1024,256]{1,0:T(8,128)S(1)}, f32[1024,256]{1,0:T(8,128)}, u32[]{:S(2)}) copy-start(f32[1024,256]{1,0:T(8,128)} %param.5) | copy-start | bytes 3145732
  0.6 128.8 %copy-start.1 = (f32[1024,256]{1,0:T(8,128)S(1)}, f32[1024,256]{1,0:T(8,128)}, u32[]{:S(2)}) copy-start(f32[1024,256]{1,0:T(8,128)} %param.4) | copy-start | bytes 3145732

commit v4 on v3

--- a/solution.py
+++ b/solution.py
@@ -16,7 +16,7 @@
 HOME = 23
 START = 0
 LAG = 4
-ADD, END = 4, 9
+ADD, END = 3, 9
 READY = (5, 10, 15, 21)
 LEVEL = ((0, 3, 1, 2, 2, 3, 3, 4), (0, 3, 3, 4, 2, 3, 1, 2), (0, 1, 3, 2, 4, 3, 3, 2))
 ONWARD = (((0, 2, 4, 5), (3,), (2, 4)), ((7,), (0, 6, 4, 7, 5), (6,)), ((1, 3), (1,), (0, 3, 7, 5)))
@@ -179,10 +179,6 @@
             def _():
                 in_y(r, q).start()
 
-    for r in range(2):
-        for n in (2 - 2 * r, 3 - 2 * r, 6 - 2 * r, 7 - 2 * r, 8, 9, 10, 11):
-            in_y(r, n).wait_recv()
-
     def slices(r, q):
         step, u = q // 4, (q + 2 * r) % 4
 
@@ -197,10 +193,6 @@
                 device_id=lines[r], device_id_type=MESH)
 
         return copy(own.at[1, at(a * 128 + u * 32, 32)]), copy(rec.at[1, at(slot(jnp.maximum(step, 1)), 32)])
-
-    for q in range(4):
-        for r in range(2):
-            slices(r, q)[0].start()
 
     for q in range(10, 14):
         gather(0, q).wait_recv()
@@ -300,7 +292,7 @@
         r_mate(g, size).start()
 
     def kept_l(g):
-        return (l + h + z + (jnp.where(g < FAR, g + 1, 0) if not isinstance(g, int) else 0)) % 2
+        return (l + h + z + (0 if isinstance(g, int) else jnp.where(g < FAR, g + 1, 0))) % 2
 
     def r_add(g, size):
         r_mate(g, size).wait_recv()
@@ -362,6 +354,15 @@
                         def _():
                             pass_on(tree, n, way, False).start()
 
+        @pl.when(t == 0)
+        def _():
+            for r in range(2):
+                for n in (2 - 2 * r, 3 - 2 * r, 6 - 2 * r, 7 - 2 * r, 8, 9, 10, 11):
+                    in_y(r, n).wait_recv()
+            for q in range(4):
+                for r in range(2):
+                    slices(r, q)[0].start()
+
         q = t // 2
 
         @pl.when(t % 2 == 0)
@@ -381,10 +382,9 @@
         def _():
             r_add(m // 8, 256)
 
-        for far in range(2):
-            @pl.when(t == 34 + 2 * far)
-            def _():
-                r_add(FAR + far, 64)
+        @pl.when((t == 34) | (t == 36))
+        def _():
+            r_add(FAR + (t - 34) // 2, 64)
 
         @pl.when((m >= 7) & (m < 31) & (m % 8 == 7))
         def _():
@@ -398,7 +398,7 @@
                 r_home(g, part)
 
         for far in range(2):
-            @pl.when(t == 39 + far)
+            @pl.when(t == 41 + far)
             def _():
                 r_sum(FAR + far, 64)
                 r_home(FAR + far, 0)
@@ -408,10 +408,10 @@
         def _():
             r_multiply(m // 8, rec.at[1, at((m // 8) * SUB, SUB)], m % 8)
 
-        for far in range(2):
-            @pl.when(t == 33 + 2 * far)
-            def _():
-                r_multiply_few(FAR + far, 64, rec.at[1, pl.ds(768 + 64 * far, 64)])
+        @pl.when((t == 33) | (t == 35))
+        def _():
+            far = (t - 33) // 2
+            r_multiply_few(FAR + far, 64, rec.at[1, at(768 + 64 * far, 64)])
 
         @pl.when(t == 2)
         def _():
@@ -432,10 +432,12 @@
         def _():
             pltpu.make_async_copy(own.at[0], rec.at[0], own_sem.at[0]).wait()
 
-        for ready in READY:
-            @pl.when((n >= ready) & (n < ready + 2))
-            def _():
-                l_multiply(READY.index(ready), n - ready)
+        group = sum((n >= ready).astype(jnp.int32) for ready in READY[1:])
+        since = n - lookup(group, READY)
+
+        @pl.when((since >= 0) & (since < 2))
+        def _():
+            l_multiply(group, since)
 
         @pl.when(one_of(n - ADD, READY))
         def _():

time: 135 us -> 134 us (level); the launches traced: 133 us -> 134 us
  no operation moved by 1% of the time
where the time goes in v4:
time: 134 us
  Pallas kernels  130 us (97%)
  other arithmetic  3.2 us (2%)
    pallas_call x1, Pallas kernels, on_device(): pl.pallas_call(kernel, out_shape=(factor, factor), in_specs=[anywhere], o...  130 us
    add x1, other arithmetic, on_device(): 0.95 * right_old + 0.05 * gram_right  3.2 us

profile of v4, /device:TPU:16, one launch (start us, length us, event | category | flops | bytes accessed | tf_op | source)
XLA Modules:
  0.0 133.9 jit_solution(6357366137660051089)
XLA Ops:
  0.6 0.0 copy-start
  0.6 0.0 copy-start.1
  0.6 130.0 %gram_factors.1 = (f32[1024,256]{1,0:T(8,128)}, f32[1024,256]{1,0:T(8,128)}) custom-call(bf16[1024,256]{1,0:T(8,128)(2,1)} %g_ref.1), custom_call_target="tpu_custom_call" | custom-call | flops 8589934592 | bytes 5242880 | tf_op jit(solution)/shard_map/gram_factors/pallas_call | solution.py:493
  130.7 0.0 copy-done
  130.7 0.0 copy-done.1
  130.7 3.2 %multiply_add_fusion = (f32[1024,256]{1,0:T(8,128)}, f32[1024,256]{1,0:T(8,128)}) fusion(f32[1024,256]{1,0:T(8,128)} %get-tuple-element.5, f32[1024,256]{1,0:T(8,128)S(1)} %copy-done, f32[1024,256]{1,0:T(8,128)} %get-tuple-element.4, f32[1024,256]{1,0:T(8,128)S(1)} %copy-done.1), kind=kLoop, calls=%fused_computation | loop fusion | flops 1572864 | bytes 6291456 | tf_op jit(solution)/shard_map/add | solution.py:514
Async XLA Ops:
  0.6 130.1 %copy-start = (f32[1024,256]{1,0:T(8,128)S(1)}, f32[1024,256]{1,0:T(8,128)}, u32[]{:S(2)}) copy-start(f32[1024,256]{1,0:T(8,128)} %param.5) | copy-start | bytes 3145732
  0.6 130.1 %copy-start.1 = (f32[1024,256]{1,0:T(8,128)S(1)}, f32[1024,256]{1,0:T(8,128)}, u32[]{:S(2)}) copy-start(f32[1024,256]{1,0:T(8,128)} %param.4) | copy-start | bytes 3145732

commit v5 on v4

--- a/solution.py
+++ b/solution.py
@@ -359,14 +359,17 @@
             for r in range(2):
                 for n in (2 - 2 * r, 3 - 2 * r, 6 - 2 * r, 7 - 2 * r, 8, 9, 10, 11):
                     in_y(r, n).wait_recv()
-            for q in range(4):
+            pass
+
+        q = t // 2
+
+        @pl.when(t % 2 == 0)
+        def _():
+            @pl.when(q < 4)
+            def _():
                 for r in range(2):
                     slices(r, q)[0].start()
 
-        q = t // 2
-
-        @pl.when(t % 2 == 0)
-        def _():
             @pl.when((q >= 4) & (q < 18))
             def _():
                 for r in range(2):

time: 134 us -> 134 us (level)
  no operation moved by 1% of the time
where the time goes in v5:
time: 134 us
  Pallas kernels  130 us (97%)
  other arithmetic  3.2 us (2%)
    pallas_call x1, Pallas kernels, on_device(): pl.pallas_call(kernel, out_shape=(factor, factor), in_specs=[anywhere], o...  130 us
    add x1, other arithmetic, on_device(): 0.95 * right_old + 0.05 * gram_right  3.2 us

profile of v5, /device:TPU:16, one launch (start us, length us, event | category | flops | bytes accessed | tf_op | source)
XLA Modules:
  0.0 134.0 jit_solution(4546106286548037452)
XLA Ops:
  0.6 0.0 copy-start
  0.6 0.0 copy-start.1
  0.6 130.1 %gram_factors.1 = (f32[1024,256]{1,0:T(8,128)}, f32[1024,256]{1,0:T(8,128)}) custom-call(bf16[1024,256]{1,0:T(8,128)(2,1)} %g_ref.1), custom_call_target="tpu_custom_call" | custom-call | flops 8589934592 | bytes 5242880 | tf_op jit(solution)/shard_map/gram_factors/pallas_call | solution.py:496
  130.8 0.0 copy-done
  130.8 0.0 copy-done.1
  130.8 3.2 %multiply_add_fusion = (f32[1024,256]{1,0:T(8,128)}, f32[1024,256]{1,0:T(8,128)}) fusion(f32[1024,256]{1,0:T(8,128)} %get-tuple-element.5, f32[1024,256]{1,0:T(8,128)S(1)} %copy-done, f32[1024,256]{1,0:T(8,128)} %get-tuple-element.4, f32[1024,256]{1,0:T(8,128)S(1)} %copy-done.1), kind=kLoop, calls=%fused_computation | loop fusion | flops 1572864 | bytes 6291456 | tf_op jit(solution)/shard_map/add | solution.py:517
Async XLA Ops:
  0.6 130.1 %copy-start = (f32[1024,256]{1,0:T(8,128)S(1)}, f32[1024,256]{1,0:T(8,128)}, u32[]{:S(2)}) copy-start(f32[1024,256]{1,0:T(8,128)} %param.5) | copy-start | bytes 3145732
  0.6 130.1 %copy-start.1 = (f32[1024,256]{1,0:T(8,128)S(1)}, f32[1024,256]{1,0:T(8,128)}, u32[]{:S(2)}) copy-start(f32[1024,256]{1,0:T(8,128)} %param.4) | copy-start | bytes 3145732
